TPU v7x, 512 devices: a whole 4x8x8 slice. The times are simulated.
512 devices in a mesh: gx: 8 (over y), gy: 8 (over z_lo, core), gz: 8 (over x, z_hi).
Axes of the slice: x: 4, y: 8, z: 8 (z_hi: 2, z_lo: 4; z = z_hi * 4 + z_lo), core: 2. Of those that a mesh axis runs over, the one named last changes fastest.
Arguments:
- inputs: bfloat16 [2048, 4096], P('gx', 'gy'), may hold values from -6 to 6
- out_grad: bfloat16 [2048, 4096], P('gx', 'gy'), may hold values from -6 to 6
- gate_act: bfloat16 [2048, 14336], P('gx', 'gz'), may hold values from -7 to 7
- up_act: bfloat16 [2048, 14336], P('gx', 'gz'), may hold values from -6 to 6
- gate_weight: bfloat16 [4096, 14336], P('gy', ('gz', 'gx')), may hold values from -0.09375 to 0.09375
- up_weight: bfloat16 [4096, 14336], P('gy', ('gz', 'gx')), may hold values from -0.09375 to 0.09375
- down_weight: bfloat16 [14336, 4096], P(('gz', 'gx'), 'gy'), may hold values from -0.046875 to 0.046875
Outputs:
- input_grad: bfloat16 [2048, 4096], P('gx', ('gy', 'gz'))
- gate_weight_grad: float32 [4096, 14336], P('gy', ('gz', 'gx'))
- up_weight_grad: float32 [4096, 14336], P('gy', ('gz', 'gx'))
- down_weight_grad: float32 [14336, 4096], P(('gz', 'gx'), 'gy')
All inputs are finite; a program needn't handle non-finite values.
Results may differ from a plain program's by a relative error of at most 0.025.
Values may be sent and summed in bfloat16 or wider, within the bound.
A program may use at most 64 MiB of HBM per device.

v0:
```python
import jax
import jax.numpy as jnp
from jax import lax
from jax.sharding import PartitionSpec as P


def derive(hidden_grad, gate_part, up_part):
    gate_full = gate_part.astype(jnp.float32)
    up_full = up_part.astype(jnp.float32)
    sigma = jax.nn.sigmoid(gate_full)
    silu_gate = gate_full * sigma
    gate_grad = (hidden_grad * up_full * sigma * (1.0 + gate_full * (1.0 - sigma))).astype(
        jnp.bfloat16
    )
    up_grad = (hidden_grad * silu_gate).astype(jnp.bfloat16)
    return (gate_grad, up_grad)


def shards(inputs, out_grad, gate_act, up_act, gate_weight, up_weight, down_weight):
    trans_dims = (((1,), (1,)), ((), ()))
    hidden_part = lax.dot_general(
        out_grad,
        lax.all_gather(down_weight, "gx", axis=0, tiled=True),
        trans_dims,
        preferred_element_type=jnp.float32,
    )
    gate_full = gate_act.astype(jnp.float32)
    hidden = (gate_full * jax.nn.sigmoid(gate_full) * up_act.astype(jnp.float32)).astype(
        jnp.bfloat16
    )
    total = lax.psum(hidden_part.astype(jnp.bfloat16), "gy").astype(jnp.float32)
    gate_grad, up_grad = derive(total, gate_act, up_act)
    pieces = (
        lax.all_gather(gate_weight, "gx", axis=1, tiled=True),
        lax.all_gather(up_weight, "gx", axis=1, tiled=True),
    )
    carry = lax.dot_general(gate_grad, pieces[0], trans_dims, preferred_element_type=jnp.float32)
    input_part = carry + lax.dot_general(
        up_grad, pieces[1], trans_dims, preferred_element_type=jnp.float32
    )
    input_grad = lax.psum_scatter(
        input_part.astype(jnp.bfloat16), "gz", scatter_dimension=1, tiled=True
    )
    stacked = jnp.stack([gate_grad, up_grad, hidden])
    owned = lax.all_to_all(stacked, "gx", split_axis=2, concat_axis=1, tiled=True)
    cols_dims = (((0,), (0,)), ((), ()))
    pieces = (
        lax.all_gather(inputs, "gx", axis=0, tiled=True),
        lax.all_gather(out_grad, "gx", axis=0, tiled=True),
    )
    gate_acc = lax.dot_general(pieces[0], owned[0], cols_dims, preferred_element_type=jnp.float32)
    up_acc = lax.dot_general(pieces[0], owned[1], cols_dims, preferred_element_type=jnp.float32)
    down_acc = lax.dot_general(owned[2], pieces[1], cols_dims, preferred_element_type=jnp.float32)
    return (input_grad, gate_acc, up_acc, down_acc)


def solution(mesh):
    in_specs = (
        P("gx", "gy"),
        P("gx", "gy"),
        P("gx", "gz"),
        P("gx", "gz"),
        P("gy", ("gz", "gx")),
        P("gy", ("gz", "gx")),
        P(("gz", "gx"), "gy"),
    )
    out_specs = (
        P("gx", ("gy", "gz")),
        P("gy", ("gz", "gx")),
        P("gy", ("gz", "gx")),
        P(("gz", "gx"), "gy"),
    )
    return jax.shard_map(shards, mesh=mesh, in_specs=in_specs, out_specs=out_specs, check_vma=False)
```

profile of v0, /device:TPU:56, one launch (start us, length us, event | category | flops | bytes accessed | tf_op | source)
XLA Modules:
  0.0 464.9 jit_solution(12538353300192025291)
XLA Ops:
  7.2 0.7 all-gather.6.cloned.1.call-update
  8.0 48.4 %all-gather.6.cloned.1.call-done = bf16[1792,512]{1,0:T(8,128)(2,1)} async-done(((bf16[224,512]{1,0:T(8,128)(2,1)}), bf16[1792,512]{1,0:T(8,128)(2,1)}) %all-gather.6.cloned.1.call-update) | async-done | bytes 1835024 | tf_op jit(solution)/shard_map/all_gather | solution.py:23
  56.4 3.2 convolution_convert_fusion
  59.6 0.7 all-gather.8.cloned.1.call-update
  60.4 0.5 all-gather.10.cloned.1.call-update
  61.0 0.5 all-gather.12.cloned.1.call-update
  61.5 77.2 %all-reduce.2.cloned.1.call-done = bf16[256,1792]{1,0:T(8,128)(2,1)} async-done(((bf16[256,1792]{1,0:T(8,128)(2,1)}), bf16[256,1792]{1,0:T(8,128)(2,1)}) %all-reduce.2.cloned.1.call-update) | async-done | bytes 917520 | tf_op jit(solution)/shard_map/psum | solution.py:31
  138.7 2.3 fusion.11
  141.0 0.9 copy-done
  142.0 0.3 pad_maximum_fusion
  142.3 4.3 copy.15
  146.6 7.3 %all-to-all-start = ((bf16[3,256,1792]{1,0,2:T(4,128)(2,1)}), bf16[3,256,1792]{1,0,2:T(4,128)(2,1)}, u32[]{:S(2)}, u32[]{:S(2)}) async-start(bf16[3,256,1792]{1,0,2:T(4,128)(2,1)} %copy.15), calls=%async_computation.1 | async-start | bytes 7340032 | tf_op jit(solution)/shard_map/all_to_all | solution.py:45
  153.9 0.5 all-gather.14.cloned.1.call-update
  154.5 65.4 %all-gather.8.cloned.1.call-done = bf16[512,1792]{0,1:T(8,128)(2,1)} async-done(((bf16[512,224]{0,1:T(8,128)(2,1)}), bf16[512,1792]{0,1:T(8,128)(2,1)}) %all-gather.8.cloned.1.call-update) | async-done | bytes 1835024 | tf_op jit(solution)/shard_map/all_gather | solution.py:34
  219.9 2.3 fusion.14
  222.2 53.1 %all-gather.10.cloned.1.call-done = bf16[512,1792]{0,1:T(8,128)(2,1)} async-done(((bf16[512,224]{0,1:T(8,128)(2,1)}), bf16[512,1792]{0,1:T(8,128)(2,1)}) %all-gather.10.cloned.1.call-update) | async-done | bytes 1835024 | tf_op jit(solution)/shard_map/all_gather | solution.py:35
  275.3 3.4 fusion.9
  278.7 2.4 copy.16
  281.7 37.3 %all-gather.12.cloned.1.call-done = bf16[2048,512]{1,0:T(8,128)(2,1)} async-done(((bf16[256,512]{1,0:T(8,128)(2,1)}), bf16[2048,512]{1,0:T(8,128)(2,1)}) %all-gather.12.cloned.1.call-update) | async-done | bytes 2097168 | tf_op jit(solution)/shard_map/all_gather | solution.py:48
  319.0 3.1 convolution_bitcast_fusion.1
  322.1 1.4 convolution_bitcast_fusion
  323.5 40.3 %all-gather.14.cloned.1.call-done = bf16[2048,512]{1,0:T(8,128)(2,1)} async-done(((bf16[256,512]{1,0:T(8,128)(2,1)}), bf16[2048,512]{1,0:T(8,128)(2,1)}) %all-gather.14.cloned.1.call-update) | async-done | bytes 2097168 | tf_op jit(solution)/shard_map/all_gather | solution.py:49
  363.9 3.0 fusion.15
  366.9 91.2 %reduce-scatter.2.cloned.1.call-done = bf16[256,64]{0,1:T(8,128)(2,1)} async-done(((bf16[256,512]{0,1:T(8,128)(2,1)}), bf16[256,64]{0,1:T(8,128)(2,1)}) %reduce-scatter.2.cloned.1.call-update) | async-done | bytes 32784 | tf_op jit(solution)/shard_map/reduce_scatter | solution.py:41
  (27 shorter events, 0.9 us)
Async XLA Ops:
  7.2 49.2 %all-gather.6.cloned.1.call-start = ((), (), s32[]{:S(2)}) async-start(), calls=%async_computation.2 | async-start | bytes 2064384 | tf_op jit(solution)/shard_map/all_gather | solution.py:23
  7.9 130.8 %copy-start.2 = (bf16[256,1792]{1,0:T(8,128)(2,1)S(1)}, bf16[256,1792]{1,0:T(8,128)(2,1)}, u32[]{:S(2)}) copy-start(bf16[256,1792]{1,0:T(8,128)(2,1)} %param.10) | copy-start | bytes 2752516
  7.9 130.8 %copy-start.3 = (bf16[256,1792]{1,0:T(8,128)(2,1)S(1)}, bf16[256,1792]{1,0:T(8,128)(2,1)}, u32[]{:S(2)}) copy-start(bf16[256,1792]{1,0:T(8,128)(2,1)} %param.9) | copy-start | bytes 2752516
  7.9 130.8 %all-reduce.2.cloned.1.call-start = ((), (), s32[]{:S(2)}) async-start(), calls=%async_computation.3 | async-start | bytes 1835008 | tf_op jit(solution)/shard_map/psum | solution.py:31
  59.6 160.3 %all-gather.8.cloned.1.call-start = ((), (), s32[]{:S(2)}) async-start(), calls=%async_computation.4 | async-start | bytes 2064384 | tf_op jit(solution)/shard_map/all_gather | solution.py:34
  60.3 214.9 %all-gather.10.cloned.1.call-start = ((), (), s32[]{:S(2)}) async-start(), calls=%async_computation.5 | async-start | bytes 2064384 | tf_op jit(solution)/shard_map/all_gather | solution.py:35
  60.9 258.1 %all-gather.12.cloned.1.call-start = ((), (), s32[]{:S(2)}) async-start(), calls=%async_computation.7 | async-start | bytes 2359296 | tf_op jit(solution)/shard_map/all_gather | solution.py:48
  141.0 0.9 copy-start
  146.6 73.3 %copy-start.1 = (bf16[256,1792]{1,0:T(8,128)(2,1)S(1)}, bf16[256,1792]{1,0:T(8,128)(2,1)}, u32[]{:S(2)}) copy-start(bf16[256,1792]{1,0:T(8,128)(2,1)} %copy-done) | copy-start | bytes 2752516
  146.6 132.1 %all-to-all-start = ((bf16[3,256,1792]{1,0,2:T(4,128)(2,1)}), bf16[3,256,1792]{1,0,2:T(4,128)(2,1)}, u32[]{:S(2)}, u32[]{:S(2)}) async-start(bf16[3,256,1792]{1,0,2:T(4,128)(2,1)} %copy.15), calls=%async_computation.1 | async-start | bytes 7340032 | tf_op jit(solution)/shard_map/all_to_all | solution.py:45
  153.9 121.4 %copy-start.4 = (bf16[256,1792]{1,0:T(8,128)(2,1)S(1)}, bf16[256,1792]{1,0:T(8,128)(2,1)}, u32[]{:S(2)}) copy-start(bf16[256,1792]{1,0:T(8,128)(2,1)} %param.9) | copy-start | bytes 2752516
  153.9 121.4 %copy-start.5 = (bf16[256,1792]{1,0:T(8,128)(2,1)S(1)}, bf16[256,1792]{1,0:T(8,128)(2,1)}, u32[]{:S(2)}) copy-start(bf16[256,1792]{1,0:T(8,128)(2,1)} %all-reduce.2.cloned.1.call-done) | copy-start | bytes 2752516
  153.9 210.0 %all-gather.14.cloned.1.call-start = ((), (), s32[]{:S(2)}) async-start(), calls=%async_computation.8 | async-start | bytes 2359296 | tf_op jit(solution)/shard_map/all_gather | solution.py:49
  154.5 303.6 %reduce-scatter.2.cloned.1.call-start = ((), (), s32[]{:S(2)}) async-start(), calls=%async_computation.6 | async-start | bytes 294912 | tf_op jit(solution)/shard_map/reduce_scatter | solution.py:41
  319.0 3.2 copy-start.6
Sparse Core Ops, SparseCore 0:
  10.1 46.2 all-gather.5
  59.7 78.9 all-reduce.1
  141.0 78.8 all-gather.7
  222.0 53.2 all-gather.9
  277.4 41.5 all-gather.11
  321.1 42.7 all-gather.13
  369.5 88.5 reduce-scatter.1
where the time goes:
time: 466 us; the launch traced here: 465 us
  waiting for transfers between devices  416 us (89%)
  matrix products  16.5 us (4%)
  between operations  14.2 us (3%)
  local copies, waits for them, and re-layouts  8.25 us (2%)
  starting transfers between devices  7.54 us (2%)
    reduce_scatter x1, waiting for transfers between devices, shards(): lax.psum_scatter(input_part.astype(jnp.bfloat16), 'gz', scatter_dimension...  91.2 us
    psum x1, waiting for transfers between devices, shards(): total = lax.psum(hidden_part.astype(jnp.bfloat16), 'gy').astype(jnp.float32)  77.2 us
    all_gather x1, waiting for transfers between devices, shards(): lax.all_gather(gate_weight, 'gx', axis=1, tiled=True)  65.4 us
    all_gather x1, waiting for transfers between devices, shards(): lax.all_gather(up_weight, 'gx', axis=1, tiled=True)  53.1 us
    all_gather x1, waiting for transfers between devices, shards(): lax.all_gather(down_weight, 'gx', axis=0, tiled=True)  48.4 us
    all_gather x1, waiting for transfers between devices, shards(): lax.all_gather(out_grad, 'gx', axis=0, tiled=True)  40.3 us
    all_gather x1, waiting for transfers between devices, shards(): lax.all_gather(inputs, 'gx', axis=0, tiled=True)  37.3 us
  transfers between devices with their start and end apart: 8, of which 7 were waited for; matrix products, arithmetic and copies ran while one was open for 5% of the time, Pallas kernels for 0%

commit v1 on v0

v1 whole, which is shorter than its diff:
```python
import jax
import jax.numpy as jnp
from jax import lax
from jax.experimental import pallas as pl
from jax.experimental.pallas import tpu as pltpu
from jax.sharding import PartitionSpec as P

MESH = pl.DeviceIdType.MESH
BF = jnp.bfloat16
F32 = jnp.float32
N = 8
ROWS = 128
SUB = 32
NT = (((1,), (1,)), ((), ()))
TN = (((0,), (0,)), ((), ()))


def kernel(
    og, inp, gact, uact, gw, uw, dw,
    out_in, out_gate, out_up, out_down,
    og_all, inp_all, gw_v, uw_v, dw_v, araw, ast, act,
    tbuf, trecv, sbuf, zrecv, grads, hid, pbuf, xrecv, fbuf, yrecv, rbuf, hrecv,
    load_sem, og_s, og_r, in_s, in_r, act_s, act_r, t_s, t_r, z_s, z_r,
    g_s, g_r, gc_s, gc_r, x_s, x_r, f_s, f_r, h_s, h_r, hc_s, hc_r, e_s, e_r,
):
    a, b, c = (lax.axis_index(n) for n in ("gx", "gy", "gz"))
    core, zl = lax.rem(b, 2), lax.div(b, 2)
    x, zh = lax.div(c, 2), lax.rem(c, 2)
    cols = dw.shape[0]

    def y_peer(step):
        return (lax.rem(a + step + N, N), b, c)

    partner = (a, b + 1 - 2 * core, c)
    far = (a, b, c + 1 - 2 * zh)

    def z_peer(i):
        return (a, 2 * lax.rem(zl + i, 4) + core, c)

    def x_peer(i):
        return (a, b, 2 * lax.rem(x + i, 4) + zh)

    def remote(src, dst, s, r, to):
        return pltpu.make_async_remote_copy(
            src_ref=src, dst_ref=dst, send_sem=s, recv_sem=r, device_id=to, device_id_type=MESH
        )

    loads = []
    for h in range(2):
        loads.append((og.at[pl.ds(h * ROWS, ROWS)], og_all.at[0, h]))
    loads.append((dw, dw_v))
    for h in range(2):
        rows = pl.ds(pl.multiple_of(h * ROWS + zl * SUB, SUB), SUB)
        loads.append((gact.at[rows], araw.at[0, h]))
        loads.append((uact.at[rows], araw.at[1, h]))
    loads.append((gw, gw_v))
    loads.append((uw, uw_v))
    for h in range(2):
        loads.append((inp.at[pl.ds(h * ROWS, ROWS)], inp_all.at[0, h]))
    loads = [pltpu.make_async_copy(s, d, load_sem.at[i]) for i, (s, d) in enumerate(loads)]
    for copy in loads:
        copy.start()

    barrier = pltpu.get_barrier_semaphore()
    peers = [y_peer(i) for i in range(1, N)] + [z_peer(i) for i in range(1, 4)]
    peers += [x_peer(i) for i in range(1, 4)] + [partner, far]
    for peer in peers:
        pl.semaphore_signal(barrier, inc=1, device_id=peer, device_id_type=MESH)
    pl.semaphore_wait(barrier, len(peers))

    def ring(buf, s, r, m, side):
        src = buf.at[0, (m - 1 + side) % 2] if isinstance(m, int) and m <= 2 else buf.at[m - 2, side]
        return remote(src, buf.at[m, side], s.at[m, side], r.at[m, side], y_peer(1 - 2 * side))

    def og_ring(m, side):
        return ring(og_all, og_s, og_r, m, side)

    def in_ring(m, side):
        return ring(inp_all, in_s, in_r, m, side)

    def act_copy(j):
        to = y_peer((1 - 2 * core) * ((j + 1) // 2))
        return remote(ast.at[to[0], lax.rem(core + j - 1, 2)], act.at[j], act_s.at[j], act_r.at[j], to)

    def t_copy(j):
        return remote(tbuf.at[j, 1 - core], trecv.at[j], t_s.at[j], t_r.at[j], partner)

    def z_copy(j, i):
        to = lax.rem(zl + i, 4)
        return remote(sbuf.at[j, to], zrecv.at[j, zl], z_s.at[j, i], z_r.at[j, i], z_peer(i))

    def g_copy(j, i):
        mine = grads.at[j, :, core, zl]
        return remote(mine, mine, g_s.at[j, i], g_r.at[j, i], z_peer(i))

    def gc_copy(j):
        mine = grads.at[j, :, core]
        return remote(mine, mine, gc_s.at[j], gc_r.at[j], partner)

    def x_copy(j, i):
        to = lax.rem(x + i, 4)
        return remote(pbuf.at[j, to], xrecv.at[j, x], x_s.at[j, i], x_r.at[j, i], x_peer(i))

    def f_copy(j, side):
        step = ((j + 1) // 2) * (2 * side - 1)
        return remote(fbuf.at[j, side], yrecv.at[j, side], f_s.at[j, side], f_r.at[j, side], y_peer(step))

    def h_copy(i):
        mine = hid.at[:, core, zl]
        return remote(mine, mine, h_s.at[i], h_r.at[i], z_peer(i))

    def hc_copy():
        mine = hid.at[:, core]
        return remote(mine, mine, hc_s.at[0], hc_r.at[0], partner)

    def e_copy():
        return remote(rbuf.at[1 - zh], hrecv, e_s.at[0], e_r.at[0], far)

    def stage_terms(j):
        term = lax.dot_general(
            og_all[j].reshape(2 * ROWS, -1), dw_v[...], NT, preferred_element_type=F32
        )
        tbuf[j] = term.astype(BF).reshape(2, ROWS, cols)
        t_copy(j).start()

    def stage_pair(j):
        t_copy(j).wait_recv()
        total = tbuf[j, core].astype(F32) + trecv[j].astype(F32)
        sbuf[j] = total.astype(BF).reshape(4, SUB, cols)
        for i in range(1, 4):
            z_copy(j, i).start()

    def stage_act(j):
        for i in range(1, 4):
            z_copy(j, i).wait_recv()
        own = sbuf[j, zl]
        zrecv[j, zl] = own
        hidden_grad = zrecv[j, 0].astype(F32)
        for i in range(1, 4):
            hidden_grad += zrecv[j, i].astype(F32)
        gate, up = act[j, 0].astype(F32), act[j, 1].astype(F32)
        sigma = jax.nn.sigmoid(gate)
        silu = gate * sigma
        grads[j, 0, core, zl] = (hidden_grad * up * sigma * (1.0 + gate * (1.0 - sigma))).astype(BF)
        grads[j, 1, core, zl] = (hidden_grad * silu).astype(BF)
        hid[j, core, zl] = (silu * up).astype(BF)
        for i in range(1, 4):
            g_copy(j, i).start()

    def stage_share(j):
        for i in range(1, 4):
            g_copy(j, i).wait_recv()
        gc_copy(j).start()

    def stage_input(j):
        gc_copy(j).wait_recv()
        part = lax.dot_general(
            grads[j, 0].reshape(2 * ROWS, cols), gw_v[...], NT, preferred_element_type=F32
        ) + lax.dot_general(
            grads[j, 1].reshape(2 * ROWS, cols), uw_v[...], NT, preferred_element_type=F32
        )
        for i in range(4):
            pbuf[j, i] = part[:, i * 128:(i + 1) * 128].astype(BF).reshape(2, ROWS, 128)
        for i in range(1, 4):
            x_copy(j, i).start()

    def stage_columns(j):
        for i in range(1, 4):
            x_copy(j, i).wait_recv()
        xrecv[j, x] = pbuf[j, x]
        total = xrecv[j, 0].astype(F32)
        for i in range(1, 4):
            total += xrecv[j, i].astype(F32)
        if isinstance(j, int) and j == 0:
            yrecv[0] = total.astype(BF)
        else:
            fbuf[j] = total.astype(BF)
            for side in range(2):
                f_copy(j, side).start()

    def stage_weights(j):
        block = inp_all[j].reshape(2 * ROWS, -1)
        gate = lax.dot_general(block, grads[j, 0].reshape(2 * ROWS, cols), TN, preferred_element_type=F32)
        up = lax.dot_general(block, grads[j, 1].reshape(2 * ROWS, cols), TN, preferred_element_type=F32)
        if isinstance(j, int) and j == 0:
            out_gate[...] = gate
            out_up[...] = up
        else:
            out_gate[...] += gate
            out_up[...] += up

    def stage_owner():
        for j in range(1, N):
            for side in range(2):
                f_copy(j, side).wait_recv()
        for half in range(2):
            total = yrecv[0, half].astype(F32)
            for j in range(1, N):
                total += yrecv[j, (j - 1 + half) % 2].astype(F32)
            for i in range(2):
                rbuf[i, pl.ds(half * ROWS, ROWS)] = total[:, i * 64:(i + 1) * 64].astype(BF)
        e_copy().start()

    for i in range(3):
        loads[i].wait()
    for m in (1, 2):
        for side in range(2):
            og_ring(m, side).start()
    stage_terms(0)
    for i in range(3, 7):
        loads[i].wait()
    for kind in range(2):
        for h in range(2):
            block = araw[kind, h]
            for i in range(N):
                ast[i, h, kind] = block[:, i * cols:(i + 1) * cols]
    act[0] = ast[a, core]
    for j in range(1, N):
        act_copy(j).start()
    stage_pair(0)

    def tick(t):
        if 1 <= t < N:
            for side in range(2):
                og_ring(t, side).wait_recv()
            if t + 2 < N:
                for side in range(2):
                    og_ring(t + 2, side).start()
            else:
                for side in range(2):
                    in_ring(t - 5, side).start()
        j = t - 7
        if 1 <= j < N:
            for side in range(2):
                in_ring(j, side).wait_recv()
            if j + 2 < N:
                for side in range(2):
                    in_ring(j + 2, side).start()
        if 0 <= t - 2 < N:
            stage_share(t - 2)
        if 1 <= t < N:
            stage_terms(t)
            act_copy(t).wait_recv()
        if 0 <= t - 1 < N:
            stage_act(t - 1)
        if t == N:
            for i in range(1, 4):
                h_copy(i).start()
        if 0 <= t - 3 < N:
            stage_columns(t - 3)
        if 1 <= t < N:
            stage_pair(t)
        if 0 <= t - 2 < N:
            stage_input(t - 2)
        if 0 <= j < N:
            stage_weights(j)
        if t == 12:
            for i in range(1, 4):
                h_copy(i).wait_recv()
            hc_copy().start()
            stage_owner()

    for copy in loads[7:]:
        copy.wait()
    for t in range(1, 15):
        tick(t)

    hc_copy().wait_recv()
    out_down[...] = lax.dot_general(
        hid[...].reshape(N * 2 * ROWS, cols), og_all[...].reshape(N * 2 * ROWS, -1), TN,
        preferred_element_type=F32,
    )
    e_copy().wait_recv()
    out_in[...] = (rbuf[zh].astype(F32) + hrecv[...].astype(F32)).astype(BF)

    for j in range(N):
        t_copy(j).wait_send()
        gc_copy(j).wait_send()
        for i in range(1, 4):
            z_copy(j, i).wait_send()
            g_copy(j, i).wait_send()
            x_copy(j, i).wait_send()
        if j >= 1:
            act_copy(j).wait_send()
            for side in range(2):
                og_ring(j, side).wait_send()
                in_ring(j, side).wait_send()
                f_copy(j, side).wait_send()
    for i in range(1, 4):
        h_copy(i).wait_send()
    hc_copy().wait_send()
    e_copy().wait_send()


def shards(inputs, out_grad, gate_act, up_act, gate_weight, up_weight, down_weight):
    width, cols = gate_weight.shape
    hidden_cols = gate_act.shape[1]
    dma = pltpu.SemaphoreType.DMA
    scratch = [
        pltpu.VMEM((N, 2, ROWS, width), BF),
        pltpu.VMEM((N, 2, ROWS, width), BF),
        pltpu.VMEM((width, cols), BF),
        pltpu.VMEM((width, cols), BF),
        pltpu.VMEM((cols, width), BF),
        pltpu.VMEM((2, 2, SUB, hidden_cols), BF),
        pltpu.VMEM((N, 2, 2, SUB, cols), BF),
        pltpu.VMEM((N, 2, SUB, cols), BF),
        pltpu.VMEM((N, 2, ROWS, cols), BF),
        pltpu.VMEM((N, ROWS, cols), BF),
        pltpu.VMEM((N, 4, SUB, cols), BF),
        pltpu.VMEM((N, 4, SUB, cols), BF),
        pltpu.VMEM((N, 2, 2, 4, SUB, cols), BF),
        pltpu.VMEM((N, 2, 4, SUB, cols), BF),
        pltpu.VMEM((N, 4, 2, ROWS, 128), BF),
        pltpu.VMEM((N, 4, 2, ROWS, 128), BF),
        pltpu.VMEM((N, 2, ROWS, 128), BF),
        pltpu.VMEM((N, 2, ROWS, 128), BF),
        pltpu.VMEM((2, 2 * ROWS, 64), BF),
        pltpu.VMEM((2 * ROWS, 64), BF),
        dma((11,)),
        dma((N, 2)), dma((N, 2)), dma((N, 2)), dma((N, 2)),
        dma((N,)), dma((N,)), dma((N,)), dma((N,)),
        dma((N, 4)), dma((N, 4)), dma((N, 4)), dma((N, 4)),
        dma((N,)), dma((N,)),
        dma((N, 4)), dma((N, 4)),
        dma((N, 2)), dma((N, 2)),
        dma((4,)), dma((4,)), dma((1,)), dma((1,)), dma((1,)), dma((1,)),
    ]
    return pl.pallas_call(
        kernel,
        out_shape=(
            jax.ShapeDtypeStruct((2 * ROWS, 64), BF),
            jax.ShapeDtypeStruct((width, cols), F32),
            jax.ShapeDtypeStruct((width, cols), F32),
            jax.ShapeDtypeStruct((cols, width), F32),
        ),
        in_specs=[pl.BlockSpec(memory_space=pl.ANY)] * 7,
        out_specs=(pl.BlockSpec(memory_space=pltpu.VMEM),) * 4,
        scratch_shapes=scratch,
        compiler_params=pltpu.CompilerParams(
            collective_id=0, has_side_effects=True, vmem_limit_bytes=56 * 1024 * 1024
        ),
        name="swiglu_backward",
    )(out_grad, inputs, gate_act, up_act, gate_weight, up_weight, down_weight)


def solution(mesh):
    in_specs = (
        P("gx", "gy"),
        P("gx", "gy"),
        P("gx", "gz"),
        P("gx", "gz"),
        P("gy", ("gz", "gx")),
        P("gy", ("gz", "gx")),
        P(("gz", "gx"), "gy"),
    )
    out_specs = (
        P("gx", ("gy", "gz")),
        P("gy", ("gz", "gx")),
        P("gy", ("gz", "gx")),
        P(("gz", "gx"), "gy"),
    )
    return jax.shard_map(shards, mesh=mesh, in_specs=in_specs, out_specs=out_specs, check_vma=False)
```

time: 466 us -> 104 us (0.22)
  the two profiles are of different devices: /device:TPU:56 before, /device:TPU:1 now
where the time goes in v1:
time: 104 us
  Pallas kernels  95.5 us (92%)
  local copies, waits for them, and re-layouts  8.05 us (8%)
    pallas_call x1, Pallas kernels, shards(): pl.pallas_call(kernel, out_shape=(jax.ShapeDtypeStruct((2 * ROWS, 64), BF...  95.5 us
    pallas_call x3, local copies, waits for them, and re-layouts, shards(): pl.pallas_call(kernel, out_shape=(jax.ShapeDtypeStruct((2 * ROWS, 64), BF...  4.56 us
    unnamed x9, local copies, waits for them, and re-layouts  3.49 us

profile of v1, /device:TPU:1, one launch (start us, length us, event | category | flops | bytes accessed | tf_op | source)
XLA Modules:
  0.0 104.2 jit_solution(4179209887003298114)
XLA Ops:
  0.6 0.0 copy-start.2
  0.6 1.8 %copy.11.gw = bf16[512,224]{1,0:T(8,128)(2,1)} copy(bf16[512,224]{0,1:T(8,128)(2,1)} %param.11) | data formatting | bytes 458752 | tf_op args[4]
  2.5 0.0 copy-done.2
  2.5 0.8 copy.12.uw
  3.3 95.5 %swiglu_backward.1 = (bf16[256,64]{1,0:T(8,128)(2,1)}, f32[512,224]{1,0:T(8,128)}, f32[512,224]{1,0:T(8,128)}, f32[224,512]{1,0:T(8,128)}) custom-call(bf16[256,512]{1,0:T(8,128)(2,1)} %og.1, bf16[256,512]{1,0:T(8,128)(2,1)} %inp.1, bf16[256,1792]{1,0:T(8,128)(2,1)} %gact.1, bf16[256,1792]{1,0:T(8,128)(2,1)} %uact.1, bf16[512,224]{1,0:T(8,128)(2,1)} %copy.11.gw, ...), custom_call_target="tpu_custom_call" | custom-call | tf_op jit(solution)/shard_map/swiglu_backward/pallas_call | solution.py:329
  98.8 0.0 copy-start
  98.8 1.6 %copy.13 = bf16[256,64]{0,1:T(8,128)(2,1)} copy(bf16[256,64]{1,0:T(8,128)(2,1)} %get-tuple-element.4) | data formatting | bytes 65536 | tf_op jit(solution)/shard_map/swiglu_backward/pallas_call | solution.py:329
  100.4 2.0 %copy.14 = f32[512,224]{0,1:T(8,128)} copy(f32[512,224]{1,0:T(8,128)} %get-tuple-element.5) | data formatting | bytes 917504 | tf_op jit(solution)/shard_map/swiglu_backward/pallas_call | solution.py:329
  102.4 0.0 copy-done
  102.4 0.0 copy-start.1
  102.4 1.0 copy.15
  103.3 0.1 copy-done.1
  103.4 0.8 copy.17
Async XLA Ops:
  0.6 1.8 %copy-start.2 = (bf16[512,224]{0,1:T(8,128)(2,1)S(1)}, bf16[512,224]{0,1:T(8,128)(2,1)}, u32[]{:S(2)}) copy-start(bf16[512,224]{0,1:T(8,128)(2,1)} %param.12) | copy-start | bytes 688132
  98.8 3.6 %copy-start = (f32[512,224]{1,0:T(8,128)S(1)}, f32[512,224]{1,0:T(8,128)}, u32[]{:S(2)}) copy-start(f32[512,224]{1,0:T(8,128)} %get-tuple-element.6) | copy-start | bytes 1376260
  102.4 1.0 copy-start.1

commit v2 on v1

--- a/solution.py
+++ b/solution.py
@@ -10,18 +10,31 @@
 F32 = jnp.float32
 N = 8
 ROWS = 128
+LAST = N - 1
 SUB = 32
 NT = (((1,), (1,)), ((), ()))
 TN = (((0,), (0,)), ((), ()))
+TIMES = (
+    (None, 2.7, 5.4, 8.1, 10.8, 13.5, 16.2, 18.9),
+    (None, 4.2, 6.9, 9.6, 12.3, 15.0, 17.7, 20.4),
+    (5.0, 8.1, 11.2, 14.3, 17.4, 20.5, 23.6, 26.7),
+    (9.2, 12.3, 15.4, 18.5, 21.6, 24.7, 27.8, 30.9),
+    (11.2, 14.3, 17.4, 20.5, 23.6, 26.7, 29.8, 32.9),
+    (15.2, 18.3, 21.4, 24.5, 27.6, 30.7, 33.8, 36.9),
+    (None, 21.6, 24.3, 27.0, 29.7, 32.4, 35.1, 37.8),
+    (19.0, 21.7, 24.4, 27.1, 29.8, 32.5, 35.2, 37.9),
+)
+ONCE = (26.8, 36.8, 39.0, 38.8, 44.9)
+ACTS_AT = {0: (1,), 1: (2,), 3: (3,), 5: (4, 5), 6: (6,), 7: (7,)}
 
 
 def kernel(
     og, inp, gact, uact, gw, uw, dw,
     out_in, out_gate, out_up, out_down,
     og_all, inp_all, gw_v, uw_v, dw_v, araw, ast, act,
-    tbuf, trecv, sbuf, zrecv, grads, hid, pbuf, xrecv, fbuf, yrecv, rbuf, hrecv,
+    tbuf, trecv, sbuf, zrecv, grads, hid, pbuf, xrecv, fbuf, yrecv, ydiag, total_in, rbuf, hrecv,
     load_sem, og_s, og_r, in_s, in_r, act_s, act_r, t_s, t_r, z_s, z_r,
-    g_s, g_r, gc_s, gc_r, x_s, x_r, f_s, f_r, h_s, h_r, hc_s, hc_r, e_s, e_r,
+    g_s, g_r, gc_s, gc_r, x_s, x_r, f_s, f_r, h_s, h_r, hc_s, hc_r, e_s, e_r, d_s, d_r,
 ):
     a, b, c = (lax.axis_index(n) for n in ("gx", "gy", "gz"))
     core, zl = lax.rem(b, 2), lax.div(b, 2)
@@ -33,6 +46,8 @@
 
     partner = (a, b + 1 - 2 * core, c)
     far = (a, b, c + 1 - 2 * zh)
+    diagonal = (lax.rem(a + N // 2, N), b, c + 1 - 2 * zh)
+    mine, other = pl.ds(pl.multiple_of(zh * 64, 64), 64), pl.ds(pl.multiple_of(64 - zh * 64, 64), 64)
 
     def z_peer(i):
         return (a, 2 * lax.rem(zl + i, 4) + core, c)
@@ -63,7 +78,7 @@
 
     barrier = pltpu.get_barrier_semaphore()
     peers = [y_peer(i) for i in range(1, N)] + [z_peer(i) for i in range(1, 4)]
-    peers += [x_peer(i) for i in range(1, 4)] + [partner, far]
+    peers += [x_peer(i) for i in range(1, 4)] + [partner, far, diagonal]
     for peer in peers:
         pl.semaphore_signal(barrier, inc=1, device_id=peer, device_id_type=MESH)
     pl.semaphore_wait(barrier, len(peers))
@@ -90,12 +105,12 @@
         return remote(sbuf.at[j, to], zrecv.at[j, zl], z_s.at[j, i], z_r.at[j, i], z_peer(i))
 
     def g_copy(j, i):
-        mine = grads.at[j, :, core, zl]
-        return remote(mine, mine, g_s.at[j, i], g_r.at[j, i], z_peer(i))
+        part = grads.at[j, :, core, zl]
+        return remote(part, part, g_s.at[j, i], g_r.at[j, i], z_peer(i))
 
     def gc_copy(j):
-        mine = grads.at[j, :, core]
-        return remote(mine, mine, gc_s.at[j], gc_r.at[j], partner)
+        part = grads.at[j, :, core]
+        return remote(part, part, gc_s.at[j], gc_r.at[j], partner)
 
     def x_copy(j, i):
         to = lax.rem(x + i, 4)
@@ -103,18 +118,24 @@
 
     def f_copy(j, side):
         step = ((j + 1) // 2) * (2 * side - 1)
-        return remote(fbuf.at[j, side], yrecv.at[j, side], f_s.at[j, side], f_r.at[j, side], y_peer(step))
+        rows = mine if j == LAST else pl.ds(0, 128)
+        return remote(
+            fbuf.at[j, side, rows], yrecv.at[j, side, rows], f_s.at[j, side], f_r.at[j, side], y_peer(step)
+        )
+
+    def d_copy(side):
+        return remote(fbuf.at[LAST, side, other], ydiag.at[side], d_s.at[side], d_r.at[side], diagonal)
 
     def h_copy(i):
-        mine = hid.at[:, core, zl]
-        return remote(mine, mine, h_s.at[i], h_r.at[i], z_peer(i))
+        part = hid.at[:, core, zl]
+        return remote(part, part, h_s.at[i], h_r.at[i], z_peer(i))
 
     def hc_copy():
-        mine = hid.at[:, core]
-        return remote(mine, mine, hc_s.at[0], hc_r.at[0], partner)
+        part = hid.at[:, core]
+        return remote(part, part, hc_s.at[0], hc_r.at[0], partner)
 
     def e_copy():
-        return remote(rbuf.at[1 - zh], hrecv, e_s.at[0], e_r.at[0], far)
+        return remote(rbuf, hrecv, e_s.at[0], e_r.at[0], far)
 
     def stage_terms(j):
         term = lax.dot_general(
@@ -154,11 +175,9 @@
 
     def stage_input(j):
         gc_copy(j).wait_recv()
-        part = lax.dot_general(
-            grads[j, 0].reshape(2 * ROWS, cols), gw_v[...], NT, preferred_element_type=F32
-        ) + lax.dot_general(
-            grads[j, 1].reshape(2 * ROWS, cols), uw_v[...], NT, preferred_element_type=F32
-        )
+        part = jnp.dot(
+            grads[j, 0].reshape(2 * ROWS, cols), gw_v[...], preferred_element_type=F32
+        ) + jnp.dot(grads[j, 1].reshape(2 * ROWS, cols), uw_v[...], preferred_element_type=F32)
         for i in range(4):
             pbuf[j, i] = part[:, i * 128:(i + 1) * 128].astype(BF).reshape(2, ROWS, 128)
         for i in range(1, 4):
@@ -171,17 +190,19 @@
         total = xrecv[j, 0].astype(F32)
         for i in range(1, 4):
             total += xrecv[j, i].astype(F32)
-        if isinstance(j, int) and j == 0:
-            yrecv[0] = total.astype(BF)
-        else:
-            fbuf[j] = total.astype(BF)
-            for side in range(2):
+        for side in range(2):
+            if j == 0:
+                yrecv[0, side] = total[side].T.astype(BF)
+            else:
+                fbuf[j, side] = total[side].T.astype(BF)
                 f_copy(j, side).start()
+                if j == LAST:
+                    d_copy(side).start()
 
     def stage_weights(j):
         block = inp_all[j].reshape(2 * ROWS, -1)
-        gate = lax.dot_general(block, grads[j, 0].reshape(2 * ROWS, cols), TN, preferred_element_type=F32)
-        up = lax.dot_general(block, grads[j, 1].reshape(2 * ROWS, cols), TN, preferred_element_type=F32)
+        gate = lax.dot_general(grads[j, 0].reshape(2 * ROWS, cols), block, TN, preferred_element_type=F32)
+        up = lax.dot_general(grads[j, 1].reshape(2 * ROWS, cols), block, TN, preferred_element_type=F32)
         if isinstance(j, int) and j == 0:
             out_gate[...] = gate
             out_up[...] = up
@@ -190,16 +211,34 @@
             out_up[...] += up
 
     def stage_owner():
-        for j in range(1, N):
+        for j in range(1, LAST):
             for side in range(2):
                 f_copy(j, side).wait_recv()
         for half in range(2):
             total = yrecv[0, half].astype(F32)
-            for j in range(1, N):
+            for j in range(1, LAST):
                 total += yrecv[j, (j - 1 + half) % 2].astype(F32)
-            for i in range(2):
-                rbuf[i, pl.ds(half * ROWS, ROWS)] = total[:, i * 64:(i + 1) * 64].astype(BF)
+            total_in[:, half * ROWS:(half + 1) * ROWS] = total
+        rbuf[...] = total_in[other].astype(BF)
         e_copy().start()
+
+    def stage_result():
+        e_copy().wait_recv()
+        for half in range(2):
+            f_copy(LAST, half).wait_recv()
+            d_copy(half).wait_recv()
+        for half in range(2):
+            cut = slice(half * ROWS, (half + 1) * ROWS)
+            total = total_in[mine, cut] + hrecv[:, cut].astype(F32)
+            total += yrecv[LAST, half, mine].astype(F32) + ydiag[half].astype(F32)
+            out_in[:, cut] = total.astype(BF)
+
+    def stage_down():
+        hc_copy().wait_recv()
+        out_down[...] = lax.dot_general(
+            hid[...].reshape(N * 2 * ROWS, cols), og_all[...].reshape(N * 2 * ROWS, -1), TN,
+            preferred_element_type=F32,
+        )
 
     for i in range(3):
         loads[i].wait()
@@ -215,63 +254,55 @@
             for i in range(N):
                 ast[i, h, kind] = block[:, i * cols:(i + 1) * cols]
     act[0] = ast[a, core]
-    for j in range(1, N):
+    for j in ACTS_AT[0]:
         act_copy(j).start()
     stage_pair(0)
 
-    def tick(t):
-        if 1 <= t < N:
-            for side in range(2):
-                og_ring(t, side).wait_recv()
-            if t + 2 < N:
-                for side in range(2):
-                    og_ring(t + 2, side).start()
-            else:
-                for side in range(2):
-                    in_ring(t - 5, side).start()
-        j = t - 7
-        if 1 <= j < N:
-            for side in range(2):
-                in_ring(j, side).wait_recv()
-            if j + 2 < N:
-                for side in range(2):
-                    in_ring(j + 2, side).start()
-        if 0 <= t - 2 < N:
-            stage_share(t - 2)
-        if 1 <= t < N:
-            stage_terms(t)
-            act_copy(t).wait_recv()
-        if 0 <= t - 1 < N:
-            stage_act(t - 1)
-        if t == N:
-            for i in range(1, 4):
-                h_copy(i).start()
-        if 0 <= t - 3 < N:
-            stage_columns(t - 3)
-        if 1 <= t < N:
-            stage_pair(t)
-        if 0 <= t - 2 < N:
-            stage_input(t - 2)
-        if 0 <= j < N:
-            stage_weights(j)
-        if t == 12:
-            for i in range(1, 4):
-                h_copy(i).wait_recv()
-            hc_copy().start()
-            stage_owner()
-
     for copy in loads[7:]:
         copy.wait()
-    for t in range(1, 15):
-        tick(t)
-
-    hc_copy().wait_recv()
-    out_down[...] = lax.dot_general(
-        hid[...].reshape(N * 2 * ROWS, cols), og_all[...].reshape(N * 2 * ROWS, -1), TN,
-        preferred_element_type=F32,
-    )
-    e_copy().wait_recv()
-    out_in[...] = (rbuf[zh].astype(F32) + hrecv[...].astype(F32)).astype(BF)
+
+    steps = []
+
+    def og_step(j):
+        for side in range(2):
+            og_ring(j, side).wait_recv()
+        for side in range(2):
+            if j + 2 < N:
+                og_ring(j + 2, side).start()
+            else:
+                in_ring(j - 5, side).start()
+        for i in ACTS_AT.get(j, ()):
+            act_copy(i).start()
+        stage_terms(j)
+
+    def in_step(j):
+        for side in range(2):
+            in_ring(j, side).wait_recv()
+        if j + 2 < N:
+            for side in range(2):
+                in_ring(j + 2, side).start()
+
+    def act_step(j):
+        if j:
+            act_copy(j).wait_recv()
+        stage_act(j)
+
+    def hid_start():
+        for i in range(1, 4):
+            h_copy(i).start()
+
+    def hid_share():
+        for i in range(1, 4):
+            h_copy(i).wait_recv()
+        hc_copy().start()
+
+    stages = (og_step, stage_pair, act_step, stage_share, stage_input, stage_columns, in_step, stage_weights)
+    for stage, times in zip(stages, TIMES, strict=True):
+        steps += [(when, stage, (j,)) for j, when in enumerate(times) if when is not None]
+    once = (hid_start, hid_share, stage_down, stage_owner, stage_result)
+    steps += [(when, step, ()) for step, when in zip(once, ONCE, strict=True)]
+    for _, step, args in sorted(steps, key=lambda s: s[0]):
+        step(*args)
 
     for j in range(N):
         t_copy(j).wait_send()
@@ -290,6 +321,21 @@
         h_copy(i).wait_send()
     hc_copy().wait_send()
     e_copy().wait_send()
+    for side in range(2):
+        d_copy(side).wait_send()
+
+
+def deliver(*refs):
+    arrays, results, held, sems = refs[0:4], refs[4:8], refs[8:12], refs[12]
+    fetch = [pltpu.make_async_copy(arrays[i], held[i], sems.at[0, i]) for i in range(4)]
+    store = [pltpu.make_async_copy(held[i], results[i], sems.at[1, i]) for i in range(4)]
+    for copy in fetch:
+        copy.start()
+    for i in range(4):
+        fetch[i].wait()
+        store[i].start()
+    for copy in store:
+        copy.wait()
 
 
 def shards(inputs, out_grad, gate_act, up_act, gate_weight, up_weight, down_weight):
@@ -299,8 +345,8 @@
     scratch = [
         pltpu.VMEM((N, 2, ROWS, width), BF),
         pltpu.VMEM((N, 2, ROWS, width), BF),
-        pltpu.VMEM((width, cols), BF),
-        pltpu.VMEM((width, cols), BF),
+        pltpu.VMEM((cols, width), BF),
+        pltpu.VMEM((cols, width), BF),
         pltpu.VMEM((cols, width), BF),
         pltpu.VMEM((2, 2, SUB, hidden_cols), BF),
         pltpu.VMEM((N, 2, 2, SUB, cols), BF),
@@ -315,8 +361,10 @@
         pltpu.VMEM((N, 4, 2, ROWS, 128), BF),
         pltpu.VMEM((N, 2, ROWS, 128), BF),
         pltpu.VMEM((N, 2, ROWS, 128), BF),
-        pltpu.VMEM((2, 2 * ROWS, 64), BF),
-        pltpu.VMEM((2 * ROWS, 64), BF),
+        pltpu.VMEM((2, 64, ROWS), BF),
+        pltpu.VMEM((128, 2 * ROWS), F32),
+        pltpu.VMEM((64, 2 * ROWS), BF),
+        pltpu.VMEM((64, 2 * ROWS), BF),
         dma((11,)),
         dma((N, 2)), dma((N, 2)), dma((N, 2)), dma((N, 2)),
         dma((N,)), dma((N,)), dma((N,)), dma((N,)),
@@ -324,14 +372,14 @@
         dma((N,)), dma((N,)),
         dma((N, 4)), dma((N, 4)),
         dma((N, 2)), dma((N, 2)),
-        dma((4,)), dma((4,)), dma((1,)), dma((1,)), dma((1,)), dma((1,)),
+        dma((4,)), dma((4,)), dma((1,)), dma((1,)), dma((1,)), dma((1,)), dma((2,)), dma((2,)),
     ]
-    return pl.pallas_call(
+    results = pl.pallas_call(
         kernel,
         out_shape=(
-            jax.ShapeDtypeStruct((2 * ROWS, 64), BF),
-            jax.ShapeDtypeStruct((width, cols), F32),
-            jax.ShapeDtypeStruct((width, cols), F32),
+            jax.ShapeDtypeStruct((64, 2 * ROWS), BF),
+            jax.ShapeDtypeStruct((cols, width), F32),
+            jax.ShapeDtypeStruct((cols, width), F32),
             jax.ShapeDtypeStruct((cols, width), F32),
         ),
         in_specs=[pl.BlockSpec(memory_space=pl.ANY)] * 7,
@@ -341,7 +389,16 @@
             collective_id=0, has_side_effects=True, vmem_limit_bytes=56 * 1024 * 1024
         ),
         name="swiglu_backward",
-    )(out_grad, inputs, gate_act, up_act, gate_weight, up_weight, down_weight)
+    )(out_grad, inputs, gate_act, up_act, gate_weight.T, up_weight.T, down_weight)
+    input_grad, gate_grad, up_grad, down_grad = pl.pallas_call(
+        deliver,
+        out_shape=tuple(jax.ShapeDtypeStruct(r.shape, r.dtype) for r in results),
+        in_specs=[pl.BlockSpec(memory_space=pl.ANY)] * 4,
+        out_specs=(pl.BlockSpec(memory_space=pl.ANY),) * 4,
+        scratch_shapes=[pltpu.VMEM(r.shape, r.dtype) for r in results] + [dma((2, 4))],
+        name="deliver",
+    )(*results)
+    return (input_grad.T, gate_grad.T, up_grad.T, down_grad)
 
 
 def solution(mesh):

time: 104 us -> 85.8 us (0.82)
  the two profiles are of different devices: /device:TPU:1 before, /device:TPU:16 now
where the time goes in v2:
time: 85.8 us; the launch traced here: 85.6 us
  Pallas kernels  85 us (99%)
    pallas_call x1, Pallas kernels, shards(): pl.pallas_call(kernel, out_shape=(jax.ShapeDtypeStruct((64, 2 * ROWS), BF...  82.8 us
    pallas_call x1, Pallas kernels, shards(): pl.pallas_call(deliver, out_shape=tuple((jax.ShapeDtypeStruct(r.shape, r....  2.18 us

profile of v2, /device:TPU:16, one launch (start us, length us, event | category | flops | bytes accessed | tf_op | source)
XLA Modules:
  0.0 85.6 jit_solution(3017186620514015558)
XLA Ops:
  0.6 82.8 %swiglu_backward.1 = (bf16[64,256]{1,0:T(8,128)(2,1)}, f32[224,512]{1,0:T(8,128)}, f32[224,512]{1,0:T(8,128)}, f32[224,512]{1,0:T(8,128)}) custom-call(bf16[256,512]{1,0:T(8,128)(2,1)} %og.1, bf16[256,512]{1,0:T(8,128)(2,1)} %inp.1, bf16[256,1792]{1,0:T(8,128)(2,1)} %gact.1, bf16[256,1792]{1,0:T(8,128)(2,1)} %uact.1, bf16[224,512]{1,0:T(8,128)(2,1)} %bitcast.5, ...), custom_call_target="tpu_custom_call" | custom-call | tf_op jit(solution)/shard_map/swiglu_backward/pallas_call | solution.py:377
  83.4 2.2 %deliver.1 = (bf16[64,256]{1,0:T(8,128)(2,1)}, f32[224,512]{1,0:T(8,128)}, f32[224,512]{1,0:T(8,128)}, f32[224,512]{1,0:T(8,128)}) custom-call(bf16[64,256]{1,0:T(8,128)(2,1)} %get-tuple-element.12.refs_0_, f32[224,512]{1,0:T(8,128)} %get-tuple-element.13.refs_1_, f32[224,512]{1,0:T(8,128)} %get-tuple-element.14.refs_2_, f32[224,512]{1,0:T(8,128)} %get-tuple-element.15.refs_3_), custom_call_target="tpu_custom_call" | custom-call | tf_op jit(solution)/shard_map/deliver/pallas_call | solution.py:393

commit v3 on v2

v3 whole, which is shorter than its diff:
```python
import jax
import jax.numpy as jnp
from jax import lax
from jax.experimental import pallas as pl
from jax.experimental.pallas import tpu as pltpu
from jax.sharding import PartitionSpec as P

MESH = pl.DeviceIdType.MESH
BF = jnp.bfloat16
F32 = jnp.float32
N = 8
ROWS = 128
LAST = N - 1
FULL = 1
SUB = 32
NT = (((1,), (1,)), ((), ()))
TN = (((0,), (0,)), ((), ()))
TIMES = (
    (None, 8.60, 11.45, 16.18, 19.26, 24.23, 28.05, 33.09),
    (9.84, 13.94, 16.79, 22.06, 26.24, 30.41, 34.98, 38.93),
    (15.68, 21.02, 25.37, 29.37, 33.69, 37.72, 42.06, 46.01),
    (24.77, 27.55, 35.90, 38.68, 41.46, 44.24, 48.25, 52.19),
    (4.80, 13.02, 21.32, 46.31, 50.09),
    (17.98, 28.25, 36.10, 58.15, 60.34),
)
ONCE = (39.03, 55.25, 57.95, 54.58, 61.78)
ACTS_AT = {0: (1,), 1: (2,), 2: (3,), 3: (4,), 4: (5,), 5: (6, 7)}


def kernel(
    og, inp, gact, uact, gw, uw, dw,
    out_in, out_gate, out_up, out_down,
    og_all, og_far, inp_all, gw_v, uw_v, dw_v, araw, ast, act,
    sbuf, zrecv, whole, grads, hid, pbuf, xrecv, fbuf, yrecv, ydiag, total_in, rbuf, hrecv,
    load_sem, swap_s, swap_r, og_s, og_r, oc_s, oc_r, in_s, in_r, ix_s, ix_r, act_s, act_r, z_s, z_r,
    g_s, g_r, gc_s, gc_r, x_s, x_r, f_s, f_r, h_s, h_r, hc_s, hc_r, e_s, e_r, d_s, d_r,
):
    a, b, c = (lax.axis_index(n) for n in ("gx", "gy", "gz"))
    core, zl = lax.rem(b, 2), lax.div(b, 2)
    x, zh = lax.div(c, 2), lax.rem(c, 2)
    cols = dw.shape[0]

    def y_peer(step):
        return (lax.rem(a + step + N, N), b, c)

    partner = (a, b + 1 - 2 * core, c)
    far = (a, b, c + 1 - 2 * zh)
    diagonal = (lax.rem(a + N // 2, N), b, c + 1 - 2 * zh)
    mine, other = pl.ds(pl.multiple_of(zh * 64, 64), 64), pl.ds(pl.multiple_of(64 - zh * 64, 64), 64)

    def z_peer(i):
        return (a, 2 * lax.rem(zl + i, 4) + core, c)

    def x_peer(i, to_core):
        return (a, 2 * zl + to_core, 2 * lax.rem(x + i, 4) + zh)

    def remote(src, dst, s, r, to):
        return pltpu.make_async_remote_copy(
            src_ref=src, dst_ref=dst, send_sem=s, recv_sem=r, device_id=to, device_id_type=MESH
        )

    loads = []
    for h in range(2):
        loads.append((og.at[pl.ds(h * ROWS, ROWS)], og_all.at[h, core]))
    for array, held in ((dw, dw_v), (gw, gw_v), (uw, uw_v)):
        loads.append((array, held.at[core]))
    for h in range(2):
        rows = pl.ds(h * ROWS, ROWS)
        loads.append((gact.at[rows], araw.at[0, h]))
        loads.append((uact.at[rows], araw.at[1, h]))
    for h in range(2):
        for q in range(2):
            loads.append((inp.at[pl.ds(h * ROWS + q * 64, 64)], inp_all.at[0, 2 * h + q]))
    loads = [pltpu.make_async_copy(s, d, load_sem.at[i]) for i, (s, d) in enumerate(loads)]
    for copy in loads:
        copy.start()

    barrier = pltpu.get_barrier_semaphore()
    peers = [y_peer(i) for i in range(1, N)] + [z_peer(i) for i in range(1, 4)]
    peers += [x_peer(i, k) for i in range(1, 4) for k in (core, 1 - core)] + [partner, far, diagonal]
    for peer in peers:
        pl.semaphore_signal(barrier, inc=1, device_id=peer, device_id_type=MESH)
    pl.semaphore_wait(barrier, len(peers))

    swaps = [og_all.at[1 - core, core], og_all.at[core, core], dw_v.at[core], gw_v.at[core], uw_v.at[core]]
    swaps = [remote(part, part, swap_s.at[i], swap_r.at[i], partner) for i, part in enumerate(swaps)]

    def half(m):
        return lax.rem(m - 1 + core, 2)

    def place(j):
        return core if j == 0 else j + 1

    def og_ring(m, k):
        src = og_all.at[half(m), k] if m <= 2 else og_all.at[m - 1, k]
        return remote(src, og_all.at[m + 1, k], og_s.at[m, k], og_r.at[m, k], y_peer(1 - 2 * core))

    def oc_copy(j):
        return remote(og_all.at[place(j), 1 - core], og_far.at[j], oc_s.at[j], oc_r.at[j], partner)

    def in_ring(d, side):
        src, dst = (d - 1, d) if side == 0 else ((N + 1 - d) % N, N - d)
        rows = pl.ds(0, 64) if d < 4 else pl.ds(32 * side, 32)
        return remote(
            inp_all.at[src, x, rows], inp_all.at[dst, x, rows], in_s.at[d, side], in_r.at[d, side],
            y_peer(1 - 2 * side),
        )

    def ix_copy(rel, i):
        part = inp_all.at[rel, x]
        return remote(part, part, ix_s.at[rel, i], ix_r.at[rel, i], x_peer(i, core))

    own_rows = pl.ds(pl.multiple_of(zl * SUB, SUB), SUB)

    def act_copy(j):
        to = y_peer((1 - 2 * core) * ((j + 1) // 2))
        rows = pl.ds(0, ROWS) if j < FULL else own_rows
        return remote(ast.at[to[0], half(j), :, rows], act.at[j, :, rows], act_s.at[j], act_r.at[j], to)

    def z_copy(j, i):
        to = lax.rem(zl + i, 4)
        return remote(sbuf.at[j, to], zrecv.at[j, zl], z_s.at[j, i], z_r.at[j, i], z_peer(i))

    def g_copy(j, i):
        part = whole.at[j, zl] if j < FULL else grads.at[j, :, core, zl]
        return remote(part, part, g_s.at[j, i], g_r.at[j, i], z_peer(i))

    def gc_copy(j):
        part = grads.at[j, :, core]
        return remote(part, part, gc_s.at[j], gc_r.at[j], partner)

    def x_copy(j, i, k):
        to, to_core = lax.rem(x + i, 4), core + k * (1 - 2 * core)
        return remote(
            pbuf.at[j, to_core, to], xrecv.at[j, x, core], x_s.at[j, i, k], x_r.at[j, i, k], x_peer(i, to_core)
        )

    def f_copy(j, side):
        step = ((j + 1) // 2) * (2 * side - 1)
        rows = mine if j == LAST else pl.ds(0, 128)
        return remote(
            fbuf.at[j, side, rows], yrecv.at[j, side, rows], f_s.at[j, side], f_r.at[j, side], y_peer(step)
        )

    def d_copy(side):
        return remote(fbuf.at[LAST, side, other], ydiag.at[side], d_s.at[side], d_r.at[side], diagonal)

    def h_copy(i):
        part = hid.at[pl.ds(FULL, N - FULL), core, zl]
        return remote(part, part, h_s.at[i], h_r.at[i], z_peer(i))

    def hc_copy():
        part = hid.at[:, core]
        return remote(part, part, hc_s.at[0], hc_r.at[0], partner)

    def e_copy():
        return remote(rbuf, hrecv, e_s.at[0], e_r.at[0], far)

    def stage_terms(j):
        term = sum(
            lax.dot_general(og_all[place(j), k], dw_v[k], NT, preferred_element_type=F32) for k in range(2)
        )
        sbuf[j] = term.astype(BF).reshape(4, SUB, cols)
        for i in range(1, 4):
            z_copy(j, i).start()
        oc_copy(j).start()

    def derive(hidden_grad, gate, up):
        sigma = jax.nn.sigmoid(gate)
        silu = gate * sigma
        gate_grad = hidden_grad * up * sigma * (1.0 + gate * (1.0 - sigma))
        return [v.astype(BF) for v in (gate_grad, hidden_grad * silu, silu * up)]

    def stage_act(j):
        for i in range(1, 4):
            z_copy(j, i).wait_recv()
        zrecv[j, zl] = sbuf[j, zl]
        hidden_grad = zrecv[j, 0].astype(F32)
        for i in range(1, 4):
            hidden_grad += zrecv[j, i].astype(F32)
        if j < FULL:
            whole[j, zl] = hidden_grad.astype(BF)
        else:
            gate, up = act[j, 0, own_rows].astype(F32), act[j, 1, own_rows].astype(F32)
            grads[j, 0, core, zl], grads[j, 1, core, zl], hid[j, core, zl] = derive(hidden_grad, gate, up)
        for i in range(1, 4):
            g_copy(j, i).start()

    def stage_input(j):
        for i in range(1, 4):
            g_copy(j, i).wait_recv()
        if j == 0:
            swaps[3].wait_recv()
            swaps[4].wait_recv()
        if j < FULL:
            gate, up = act[j, 0].astype(F32), act[j, 1].astype(F32)
            block = (4, SUB, cols)
            values = derive(whole[j].reshape(ROWS, cols).astype(F32), gate, up)
            grads[j, 0, core], grads[j, 1, core], hid[j, core] = [v.reshape(block) for v in values]
        gate, up = grads[j, 0, core].reshape(ROWS, cols), grads[j, 1, core].reshape(ROWS, cols)
        for k in range(2):
            part = jnp.dot(gate, gw_v[k], preferred_element_type=F32)
            part += jnp.dot(up, uw_v[k], preferred_element_type=F32)
            for i in range(4):
                pbuf[j, k, i] = part[:, i * 128:(i + 1) * 128].astype(BF)
        for i in range(1, 4):
            for k in range(2):
                x_copy(j, i, k).start()
        x_copy(j, 0, 1).start()
        gc_copy(j).start()

    def stage_columns(j):
        x_copy(j, 0, 1).wait_recv()
        for i in range(1, 4):
            for k in range(2):
                x_copy(j, i, k).wait_recv()
        xrecv[j, x, core] = pbuf[j, core, x]
        total = xrecv[j, 0].astype(F32)
        for i in range(1, 4):
            total += xrecv[j, i].astype(F32)
        for side in range(2):
            if j == 0:
                yrecv[0, side] = total[side].T.astype(BF)
            else:
                fbuf[j, side] = total[side].T.astype(BF)
                f_copy(j, side).start()
                if j == LAST:
                    d_copy(side).start()

    def stage_weights(d):
        for j in sorted({max(2 * d - 1, 0), min(2 * d, LAST)}):
            gc_copy(j).wait_recv()
        for rel in sorted({d, (N - d) % N}):
            if rel:
                for i in range(1, 4):
                    ix_copy(rel, i).wait_recv()
            if rel in (0, 4):
                halves = ((max(2 * d - 1, 0), 0), (max(2 * d - 1, 0), 1))
            elif rel < 4:
                halves = ((2 * d - 1, 0), (2 * d, 0))
            else:
                halves = ((2 * d, 1), (2 * d - 1, 1))
            block = inp_all[rel].reshape(2 * ROWS, -1)
            for kind, out in enumerate((out_gate, out_up)):
                part = jnp.concatenate([grads[j, kind, side].reshape(ROWS, cols) for j, side in halves])
                term = lax.dot_general(part, block, TN, preferred_element_type=F32)
                out[...] = out[...] + term if rel else term

    def stage_owner():
        for j in range(1, LAST):
            for side in range(2):
                f_copy(j, side).wait_recv()
        for half in range(2):
            total = yrecv[0, half].astype(F32)
            for j in range(1, LAST):
                total += yrecv[j, (j - 1 + half) % 2].astype(F32)
            total_in[:, half * ROWS:(half + 1) * ROWS] = total
        rbuf[...] = total_in[other].astype(BF)
        e_copy().start()

    def stage_result():
        e_copy().wait_recv()
        for half in range(2):
            f_copy(LAST, half).wait_recv()
            d_copy(half).wait_recv()
        for half in range(2):
            cut = slice(half * ROWS, (half + 1) * ROWS)
            total = total_in[mine, cut] + hrecv[:, cut].astype(F32)
            total += yrecv[LAST, half, mine].astype(F32) + ydiag[half].astype(F32)
            out_in[:, cut] = total.astype(BF)

    def stage_down():
        hc_copy().wait_recv()
        for j in range(N):
            oc_copy(j).wait_recv()
        near = jnp.concatenate([og_all[place(j), core] for j in range(N)])
        far_block = og_far[...].reshape(N * ROWS, -1)
        total = lax.dot_general(
            hid[:, core].reshape(N * ROWS, cols), near, TN, preferred_element_type=F32
        ) + lax.dot_general(
            hid[:, 1 - core].reshape(N * ROWS, cols), far_block, TN, preferred_element_type=F32
        )
        out_down[...] = total

    loads[0].wait()
    loads[1].wait()
    swaps[0].start()
    og_ring(1, core).start()
    swaps[1].start()
    og_ring(2, core).start()
    for load, swap in zip(loads[2:5], swaps[2:]):
        load.wait()
        swap.start()
    swaps[0].wait_recv()
    og_ring(1, 1 - core).start()
    swaps[1].wait_recv()
    og_ring(2, 1 - core).start()
    swaps[2].wait_recv()
    stage_terms(0)
    for i in range(5, 9):
        loads[i].wait()
    for h in range(2):
        for kind in range(2):
            block = araw[kind, h]
            for i in range(N):
                ast[i, h, kind] = block[:, i * cols:(i + 1) * cols]
    act[0] = ast[a, core]
    for j in ACTS_AT[0]:
        act_copy(j).start()
    for copy in loads[9:]:
        copy.wait()

    steps = []

    def og_step(j):
        for k in range(2):
            og_ring(j, k).wait_recv()
        for k in range(2):
            if j + 2 < N:
                og_ring(j + 2, k).start()
        for i in ACTS_AT.get(j, ()):
            act_copy(i).start()
        stage_terms(j)

    def in_step(d):
        if d:
            for side in range(2):
                in_ring(d, side).wait_recv()
        if d < 4:
            for side in range(2):
                in_ring(d + 1, side).start()
        for rel in sorted({d, (N - d) % N} - {0}):
            for i in range(1, 4):
                ix_copy(rel, i).start()

    def act_step(j):
        if j:
            act_copy(j).wait_recv()
        stage_act(j)

    def hid_start():
        for i in range(1, 4):
            h_copy(i).start()

    def hid_share():
        for i in range(1, 4):
            h_copy(i).wait_recv()
        hc_copy().start()

    stages = (og_step, act_step, stage_input, stage_columns, in_step, stage_weights)
    for stage, times in zip(stages, TIMES, strict=True):
        steps += [(when, stage, (j,)) for j, when in enumerate(times) if when is not None]
    once = (hid_start, hid_share, stage_down, stage_owner, stage_result)
    steps += [(when, step, ()) for step, when in zip(once, ONCE, strict=True)]
    for _, step, args in sorted(steps, key=lambda s: s[0]):
        step(*args)

    for j in range(N):
        oc_copy(j).wait_send()
        gc_copy(j).wait_send()
        x_copy(j, 0, 1).wait_send()
        for i in range(1, 4):
            z_copy(j, i).wait_send()
            g_copy(j, i).wait_send()
            for k in range(2):
                x_copy(j, i, k).wait_send()
        if j >= 1:
            act_copy(j).wait_send()
            for side in range(2):
                og_ring(j, side).wait_send()
                f_copy(j, side).wait_send()
    for i in range(1, 4):
        h_copy(i).wait_send()
    for swap in swaps:
        swap.wait_send()
    hc_copy().wait_send()
    e_copy().wait_send()
    for side in range(2):
        d_copy(side).wait_send()
        for d in range(1, 5):
            in_ring(d, side).wait_send()
    for rel in range(1, N):
        for i in range(1, 4):
            ix_copy(rel, i).wait_send()


def deliver(*refs):
    arrays, results, held, sems = refs[0:4], refs[4:8], refs[8:12], refs[12]
    fetch = [pltpu.make_async_copy(arrays[i], held[i], sems.at[0, i]) for i in range(4)]
    store = [pltpu.make_async_copy(held[i], results[i], sems.at[1, i]) for i in range(4)]
    for copy in fetch:
        copy.start()
    for i in range(4):
        fetch[i].wait()
        store[i].start()
    for copy in store:
        copy.wait()


def shards(inputs, out_grad, gate_act, up_act, gate_weight, up_weight, down_weight):
    width, cols = gate_weight.shape
    hidden_cols = gate_act.shape[1]
    dma = pltpu.SemaphoreType.DMA
    scratch = [
        pltpu.VMEM((N + 1, 2, ROWS, width), BF),
        pltpu.VMEM((N, ROWS, width), BF),
        pltpu.VMEM((N, 4, ROWS // 2, width), BF),
        pltpu.VMEM((2, cols, width), BF),
        pltpu.VMEM((2, cols, width), BF),
        pltpu.VMEM((2, cols, width), BF),
        pltpu.VMEM((2, 2, ROWS, hidden_cols), BF),
        pltpu.VMEM((N, 2, 2, ROWS, cols), BF),
        pltpu.VMEM((N, 2, ROWS, cols), BF),
        pltpu.VMEM((N, 4, SUB, cols), BF),
        pltpu.VMEM((N, 4, SUB, cols), BF),
        pltpu.VMEM((N, 4, SUB, cols), BF),
        pltpu.VMEM((N, 2, 2, 4, SUB, cols), BF),
        pltpu.VMEM((N, 2, 4, SUB, cols), BF),
        pltpu.VMEM((N, 2, 4, ROWS, 128), BF),
        pltpu.VMEM((N, 4, 2, ROWS, 128), BF),
        pltpu.VMEM((N, 2, ROWS, 128), BF),
        pltpu.VMEM((N, 2, ROWS, 128), BF),
        pltpu.VMEM((2, 64, ROWS), BF),
        pltpu.VMEM((128, 2 * ROWS), F32),
        pltpu.VMEM((64, 2 * ROWS), BF),
        pltpu.VMEM((64, 2 * ROWS), BF),
        dma((13,)), dma((5,)), dma((5,)),
        dma((N, 2)), dma((N, 2)), dma((N,)), dma((N,)), dma((5, 2)), dma((5, 2)), dma((N, 4)), dma((N, 4)),
        dma((N,)), dma((N,)),
        dma((N, 4)), dma((N, 4)), dma((N, 4)), dma((N, 4)),
        dma((N,)), dma((N,)),
        dma((N, 4, 2)), dma((N, 4, 2)),
        dma((N, 2)), dma((N, 2)),
        dma((4,)), dma((4,)), dma((1,)), dma((1,)), dma((1,)), dma((1,)), dma((2,)), dma((2,)),
    ]
    results = pl.pallas_call(
        kernel,
        out_shape=(
            jax.ShapeDtypeStruct((64, 2 * ROWS), BF),
            jax.ShapeDtypeStruct((cols, width), F32),
            jax.ShapeDtypeStruct((cols, width), F32),
            jax.ShapeDtypeStruct((cols, width), F32),
        ),
        in_specs=[pl.BlockSpec(memory_space=pl.ANY)] * 7,
        out_specs=(pl.BlockSpec(memory_space=pltpu.VMEM),) * 4,
        scratch_shapes=scratch,
        compiler_params=pltpu.CompilerParams(
            collective_id=0, has_side_effects=True, vmem_limit_bytes=56 * 1024 * 1024
        ),
        name="swiglu_backward",
    )(out_grad, inputs, gate_act, up_act, gate_weight.T, up_weight.T, down_weight)
    input_grad, gate_grad, up_grad, down_grad = pl.pallas_call(
        deliver,
        out_shape=tuple(jax.ShapeDtypeStruct(r.shape, r.dtype) for r in results),
        in_specs=[pl.BlockSpec(memory_space=pl.ANY)] * 4,
        out_specs=(pl.BlockSpec(memory_space=pl.ANY),) * 4,
        scratch_shapes=[pltpu.VMEM(r.shape, r.dtype) for r in results] + [dma((2, 4))],
        name="deliver",
    )(*results)
    return (input_grad.T, gate_grad.T, up_grad.T, down_grad)


def solution(mesh):
    in_specs = (
        P("gx", "gy"),
        P("gx", "gy"),
        P("gx", "gz"),
        P("gx", "gz"),
        P("gy", ("gz", "gx")),
        P("gy", ("gz", "gx")),
        P(("gz", "gx"), "gy"),
    )
    out_specs = (
        P("gx", ("gy", "gz")),
        P("gy", ("gz", "gx")),
        P("gy", ("gz", "gx")),
        P(("gz", "gx"), "gy"),
    )
    return jax.shard_map(shards, mesh=mesh, in_specs=in_specs, out_specs=out_specs, check_vma=False)
```

time: 85.8 us -> 82.6 us (0.963)
  the two profiles are of different devices: /device:TPU:16 before, /device:TPU:56 now
where the time goes in v3:
time: 82.6 us; the launch traced here: 82.4 us
  Pallas kernels  81.8 us (99%)
    pallas_call x1, Pallas kernels, shards(): pl.pallas_call(kernel, out_shape=(jax.ShapeDtypeStruct((64, 2 * ROWS), BF...  79.6 us
    pallas_call x1, Pallas kernels, shards(): pl.pallas_call(deliver, out_shape=tuple((jax.ShapeDtypeStruct(r.shape, r....  2.18 us

profile of v3, /device:TPU:56, one launch (start us, length us, event | category | flops | bytes accessed | tf_op | source)
XLA Modules:
  0.0 82.4 jit_solution(15925991504505855103)
XLA Ops:
  0.6 79.6 %swiglu_backward.1 = (bf16[64,256]{1,0:T(8,128)(2,1)}, f32[224,512]{1,0:T(8,128)}, f32[224,512]{1,0:T(8,128)}, f32[224,512]{1,0:T(8,128)}) custom-call(bf16[256,512]{1,0:T(8,128)(2,1)} %og.1, bf16[256,512]{1,0:T(8,128)(2,1)} %inp.1, bf16[256,1792]{1,0:T(8,128)(2,1)} %gact.1, bf16[256,1792]{1,0:T(8,128)(2,1)} %uact.1, bf16[224,512]{1,0:T(8,128)(2,1)} %bitcast.5, ...), custom_call_target="tpu_custom_call" | custom-call | tf_op jit(solution)/shard_map/swiglu_backward/pallas_call | solution.py:436
  80.3 2.2 %deliver.1 = (bf16[64,256]{1,0:T(8,128)(2,1)}, f32[224,512]{1,0:T(8,128)}, f32[224,512]{1,0:T(8,128)}, f32[224,512]{1,0:T(8,128)}) custom-call(bf16[64,256]{1,0:T(8,128)(2,1)} %get-tuple-element.12.refs_0_, f32[224,512]{1,0:T(8,128)} %get-tuple-element.13.refs_1_, f32[224,512]{1,0:T(8,128)} %get-tuple-element.14.refs_2_, f32[224,512]{1,0:T(8,128)} %get-tuple-element.15.refs_3_), custom_call_target="tpu_custom_call" | custom-call | tf_op jit(solution)/shard_map/deliver/pallas_call | solution.py:452

commit v4 on v3

--- a/solution.py
+++ b/solution.py
@@ -16,15 +16,15 @@
 NT = (((1,), (1,)), ((), ()))
 TN = (((0,), (0,)), ((), ()))
 TIMES = (
-    (None, 8.60, 11.45, 16.18, 19.26, 24.23, 28.05, 33.09),
-    (9.84, 13.94, 16.79, 22.06, 26.24, 30.41, 34.98, 38.93),
-    (15.68, 21.02, 25.37, 29.37, 33.69, 37.72, 42.06, 46.01),
-    (24.77, 27.55, 35.90, 38.68, 41.46, 44.24, 48.25, 52.19),
-    (4.80, 13.02, 21.32, 46.31, 50.09),
-    (17.98, 28.25, 36.10, 58.15, 60.34),
+    (None, 8.90, 11.75, 16.48, 19.56, 24.53, 28.35, 33.39),
+    (9.84, 14.24, 17.09, 22.36, 26.54, 30.71, 35.28, 39.23),
+    (15.98, 21.32, 25.67, 29.67, 33.99, 38.02, 42.36, 46.31),
+    (25.07, 27.85, 36.20, 38.98, 41.76, 44.54, 48.55, 52.49),
+    (4.80, 13.32, 21.62, 46.61, 50.69),
+    (18.28, 28.55, 36.40, 58.45, 60.64),
 )
-ONCE = (39.03, 55.25, 57.95, 54.58, 61.78)
-ACTS_AT = {0: (1,), 1: (2,), 2: (3,), 3: (4,), 4: (5,), 5: (6, 7)}
+ONCE = (39.33, 55.55, 58.25, 55.18, 62.38)
+ACTS_AT = {0: (1,), 1: (2,), 2: (3,), 3: (4,), 4: (5,), 5: (6,), 6: (7,)}
 
 
 def kernel(

time: 82.6 us -> 82.6 us (level)
  no operation moved by 1% of the time
where the time goes in v4:
time: 82.6 us; the launch traced here: 82.4 us
  Pallas kernels  81.8 us (99%)
    pallas_call x1, Pallas kernels, shards(): pl.pallas_call(kernel, out_shape=(jax.ShapeDtypeStruct((64, 2 * ROWS), BF...  79.6 us
    pallas_call x1, Pallas kernels, shards(): pl.pallas_call(deliver, out_shape=tuple((jax.ShapeDtypeStruct(r.shape, r....  2.18 us

profile of v4, /device:TPU:56, one launch (start us, length us, event | category | flops | bytes accessed | tf_op | source)
XLA Modules:
  0.0 82.4 jit_solution(8760016371282776853)
XLA Ops:
  0.6 79.6 %swiglu_backward.1 = (bf16[64,256]{1,0:T(8,128)(2,1)}, f32[224,512]{1,0:T(8,128)}, f32[224,512]{1,0:T(8,128)}, f32[224,512]{1,0:T(8,128)}) custom-call(bf16[256,512]{1,0:T(8,128)(2,1)} %og.1, bf16[256,512]{1,0:T(8,128)(2,1)} %inp.1, bf16[256,1792]{1,0:T(8,128)(2,1)} %gact.1, bf16[256,1792]{1,0:T(8,128)(2,1)} %uact.1, bf16[224,512]{1,0:T(8,128)(2,1)} %bitcast.5, ...), custom_call_target="tpu_custom_call" | custom-call | tf_op jit(solution)/shard_map/swiglu_backward/pallas_call | solution.py:436
  80.3 2.2 %deliver.1 = (bf16[64,256]{1,0:T(8,128)(2,1)}, f32[224,512]{1,0:T(8,128)}, f32[224,512]{1,0:T(8,128)}, f32[224,512]{1,0:T(8,128)}) custom-call(bf16[64,256]{1,0:T(8,128)(2,1)} %get-tuple-element.12.refs_0_, f32[224,512]{1,0:T(8,128)} %get-tuple-element.13.refs_1_, f32[224,512]{1,0:T(8,128)} %get-tuple-element.14.refs_2_, f32[224,512]{1,0:T(8,128)} %get-tuple-element.15.refs_3_), custom_call_target="tpu_custom_call" | custom-call | tf_op jit(solution)/shard_map/deliver/pallas_call | solution.py:452
